TPU v7x, 32 devices: a whole 2x2x4 slice. The times are simulated.
32 devices in a mesh: pole: 4 (over y, x), row: 2 (over core), col: 4 (over z).
Axes of the slice: x: 2, y: 2, z: 4, core: 2. Of those that a mesh axis runs over, the one named last changes fastest.
Arguments:
- hamiltonian_panel: bfloat16 [6144, 512], P(('row', 'col'), 'pole'), may hold values from -0.005859375 to 0.005859375
- margin_panel: bfloat16 [6144, 512], P(('row', 'col'), 'pole'), may hold values from -0.0029296875 to 0.0029296875
- shifts: float32 [4, 2], P('pole'), may hold values from -2 to 2
- weights: float32 [4, 2], P('pole'), may hold values from 0.5 to 2
- pivot_inverse: float32 [4, 2, 512, 512], P('pole'), may hold values from -6 to 6
- selected_inverse: bfloat16 [4, 2, 6144, 6144], P('pole', None, 'row', 'col'), may hold values from -6 to 6
Outputs:
- inverse_column: float32 [4, 6144, 2, 512], P('pole', ('row', 'col'))
- inverse_pivot: float32 [4, 2, 512, 512], P('pole')
- density_column: float32 [6144, 512], P(('row', 'col'), 'pole')
- density_pivot: float32 [512, 512], P('pole')
All inputs are finite; a program needn't handle non-finite values.
Results may differ from a plain program's by a relative error of at most 0.0037.
Values may be sent and summed in bfloat16 or wider, within the bound.
A program may use at most 128 MiB of HBM per device.

v0:
```python
import jax
import jax.numpy as jnp
from jax import lax
from jax.sharding import PartitionSpec as P

HALVES = 2


def precise(left, right):
    return jnp.dot(left, right, precision=lax.Precision.HIGH, preferred_element_type=jnp.float32)


def gather_panel(pair):
    rows = pair.shape[0] // 2
    return (
        lax.all_gather(pair[:rows], "pole", axis=1, tiled=True),
        lax.all_gather(pair[rows:], "pole", axis=1, tiled=True),
    )


def exchange_sum(pieces, axis):
    return jnp.sum(lax.all_to_all(pieces, axis, 0, 0, tiled=True).astype(jnp.float32), axis=0)


def factor_panel(pair, shift, inverse):
    hamiltonian_f = pair[0].astype(jnp.float32)
    margin_f = pair[1].astype(jnp.float32)
    real_part = hamiltonian_f - shift[0] * margin_f
    imag_part = -shift[1] * margin_f
    lower_real = precise(real_part, inverse[0]) - precise(imag_part, inverse[1])
    lower_imag = precise(real_part, inverse[1]) + precise(imag_part, inverse[0])
    return (lower_real.astype(jnp.bfloat16), lower_imag.astype(jnp.bfloat16))


def half_dot(left, right):
    return lax.dot_general(
        left, right, (((0,), (0,)), ((), ())), preferred_element_type=jnp.float32
    )


def body(hamiltonian_panel, margin_panel, shifts, weights, pivot_inverse, selected_inverse):
    shift = shifts[0]
    weight = weights[0]
    inverse = pivot_inverse[0]
    block_real = selected_inverse[0, 0]
    block_imag = selected_inverse[0, 1]
    n_row = lax.axis_size("row")
    n_col = lax.axis_size("col")
    n_pole = lax.axis_size("pole")
    width = inverse.shape[-1]
    part = width // HALVES
    own_pair = jnp.concatenate([hamiltonian_panel, margin_panel], axis=0)
    order = [(n_row * c + r, r * n_col + c) for r in range(n_row) for c in range(n_col)]
    met_pair = gather_panel(lax.ppermute(own_pair, ("row", "col"), order))
    met_real, met_imag = factor_panel(met_pair, shift, inverse)
    partials = []
    for h in range(HALVES):
        cut = slice(h * part, (h + 1) * part)
        mine = jnp.concatenate([met_real[:, cut], met_imag[:, cut]], axis=1)
        rows = lax.all_gather(mine, "row", axis=0, tiled=True)
        turned = jnp.concatenate([rows[:, part:], -rows[:, :part]], axis=1)
        total = jnp.dot(block_imag, turned, preferred_element_type=jnp.float32) - jnp.dot(
            block_real, rows, preferred_element_type=jnp.float32
        )
        partials.append(total.astype(jnp.bfloat16))
    own_pair, partials[-1] = lax.optimization_barrier((own_pair, partials[-1]))
    own_real, own_imag = factor_panel(gather_panel(own_pair), shift, inverse)
    lower = jnp.concatenate([own_real, own_imag], axis=1)
    columns = []
    updates = []
    for h in range(HALVES):
        column = exchange_sum(partials[h].reshape(n_col, -1, 2 * part), "col")
        high = column.astype(jnp.bfloat16)
        low = (column - high.astype(jnp.float32)).astype(jnp.bfloat16)
        square = half_dot(lower, high) + half_dot(lower, low)
        update = jnp.stack(
            [
                square[:width, :part] - square[width:, part:],
                square[:width, part:] + square[width:, :part],
            ]
        )
        updates.append(update)
        columns.append(column.reshape(column.shape[0], 2, part))
    column = jnp.concatenate(columns, axis=2)
    update = jnp.concatenate(updates, axis=2)
    pieces = update.reshape(n_row * n_col, -1, width).astype(jnp.bfloat16)
    piece = lax.optimization_barrier(exchange_sum(pieces, ("row", "col")))
    update = lax.all_gather(piece.astype(jnp.bfloat16), ("row", "col"), axis=0, tiled=True)
    pivot = inverse - update.reshape(2, width, width).astype(jnp.float32)
    column_density = weight[0] * column[:, 0] - weight[1] * column[:, 1]
    share = width // n_pole
    column_share = exchange_sum(column_density.reshape(-1, n_pole, share).swapaxes(0, 1), "pole")
    pivot_density = weight[0] * pivot[0] - weight[1] * pivot[1]
    pivot_share = exchange_sum(pivot_density.reshape(n_pole, share, width), "pole")
    return (column[None], pivot[None], column_share, pivot_share)


def solution(mesh):
    return jax.shard_map(
        body,
        mesh=mesh,
        in_specs=(
            P(("row", "col"), "pole"),
            P(("row", "col"), "pole"),
            P("pole", None),
            P("pole", None),
            P("pole", None, None, None),
            P("pole", None, "row", "col"),
        ),
        out_specs=(
            P("pole", ("row", "col"), None, None),
            P("pole", None, None, None),
            P(("row", "col"), "pole"),
            P("pole", None),
        ),
        check_vma=False,
    )
```

profile of v0, /device:TPU:0, one launch (start us, length us, event | category | flops | bytes accessed | tf_op | source)
XLA Modules:
  0.0 332.2 jit_solution(18348677781217761953)
XLA Ops:
  7.2 1.1 constant_dynamic-update-slice_fusion.1
  10.0 1.3 fusion.91
  12.0 12.6 %all_gather.22 = bf16[768,512]{1,0:T(8,128)(2,1)S(1)} all-gather(bf16[768,128]{1,0:T(8,128)(2,1)S(1)} %get-tuple-element.27), channel_id=1, replica_groups=mesh['pole'=4,'row'=2,'col'=4] {'pole'}, dimensions={1}, use_global_device_ids=true | all-gather | bytes 983040 | tf_op jit(solution)/shard_map/all_gather | solution.py:17
  24.5 1.6 fusion.21
  26.2 1.6 fusion.20
  27.8 12.2 %all_gather.21 = bf16[768,512]{1,0:T(8,128)(2,1)S(1)} all-gather(bf16[768,128]{1,0:T(8,128)(2,1)S(1)} %get-tuple-element.26), channel_id=1, replica_groups=mesh['pole'=4,'row'=2,'col'=4] {'pole'}, dimensions={1}, use_global_device_ids=true | all-gather | bytes 983040 | tf_op jit(solution)/shard_map/all_gather | solution.py:16
  40.0 2.3 subtract_convert_fusion.5
  42.3 2.3 add_convert_fusion.1
  45.7 19.8 %all-gather.6.cloned.1.call-done = bf16[1536,512]{0,1:T(8,128)(2,1)} async-done(((bf16[768,512]{0,1:T(8,128)(2,1)}), bf16[1536,512]{0,1:T(8,128)(2,1)}) %all-gather.6.cloned.1.call-update) | async-done | bytes 1572880 | tf_op jit(solution)/shard_map/all_gather | solution.py:60
  65.5 1.6 fusion.85
  67.4 7.7 %fusion = f32[512,3072]{1,0:T(8,128)S(1)} fusion(bf16[1536,512]{0,1:T(8,128)(2,1)S(1)} %copy-done.6, bf16[1,2,3072,1536]{3,2,1,0:T(8,128)(2,1)} %param.11), kind=kOutput, calls=%fused_computation | convolution fusion | flops 4831838208 | bytes 17301504 | tf_op jit(solution)/shard_map/dot_general | solution.py:62
  75.1 7.6 %fusion.16 = bf16[3072,512]{0,1:T(8,128)(2,1)S(1)} fusion(f32[512,3072]{1,0:T(8,128)S(1)} %fusion, bf16[1,2,3072,1536]{3,2,1,0:T(8,128)(2,1)} %param.11, bf16[1536,256]{0,1:T(8,128)(2,1)S(1)} %get-tuple-element.19, bf16[1536,256]{0,1:T(8,128)(2,1)S(1)} %get-tuple-element.18), kind=kOutput, calls=%fused_computation.21 | convolution fusion | flops 4838129664 | bytes 20447232 | tf_op jit(solution)/shard_map/dot_general | solution.py:62
  82.7 1.9 copy.31
  84.6 4.9 %all-to-all-start.1 = ((bf16[4,768,512]{1,2,0:T(8,128)(2,1)}), bf16[4,768,512]{1,2,0:T(8,128)(2,1)}, u32[]{:S(2)}, u32[]{:S(2)}) async-start(bf16[4,768,512]{1,2,0:T(8,128)(2,1)} %bitcast.79), calls=%async_computation.1 | async-start | bytes 6291456 | tf_op jit(solution)/shard_map/all_to_all | solution.py:22
  90.4 13.2 %all-gather.4.cloned.1.call-done = bf16[1536,512]{0,1:T(8,128)(2,1)} async-done(((bf16[768,512]{0,1:T(8,128)(2,1)}), bf16[1536,512]{0,1:T(8,128)(2,1)}) %all-gather.4.cloned.1.call-update) | async-done | bytes 1572880 | tf_op jit(solution)/shard_map/all_gather | solution.py:60
  103.7 1.6 fusion.84
  105.5 7.7 %fusion.2 = f32[512,3072]{1,0:T(8,128)S(1)} fusion(bf16[1536,512]{0,1:T(8,128)(2,1)S(1)} %copy-done.7, bf16[1,2,3072,1536]{3,2,1,0:T(8,128)(2,1)} %param.11), kind=kOutput, calls=%fused_computation.2 | convolution fusion | flops 4831838208 | bytes 17301504 | tf_op jit(solution)/shard_map/dot_general | solution.py:62
  113.2 7.6 %subtract_convert_fusion.1 = bf16[512,3072]{1,0:T(8,128)(2,1)S(1)} fusion(f32[512,3072]{1,0:T(8,128)S(1)} %fusion.2, bf16[1,2,3072,1536]{3,2,1,0:T(8,128)(2,1)} %param.11, bf16[1536,256]{0,1:T(8,128)(2,1)S(1)} %get-tuple-element.17, bf16[1536,256]{0,1:T(8,128)(2,1)S(1)} %get-tuple-element.16), kind=kOutput, calls=%fused_computation.15 | convolution fusion | flops 4838129664 | bytes 20447232 | tf_op jit(solution)/shard_map/dot_general | solution.py:62
  120.9 1.9 copy.32
  122.8 38.0 %all-to-all-done.1 = bf16[4,768,512]{1,2,0:T(8,128)(2,1)} async-done(((bf16[4,768,512]{1,2,0:T(8,128)(2,1)}), bf16[4,768,512]{1,2,0:T(8,128)(2,1)}, u32[]{:S(2)}, u32[]{:S(2)}) %all-to-all-start.1) | async-done | bytes 3145760 | tf_op jit(solution)/shard_map/all_to_all | solution.py:22
  160.8 4.7 %all-to-all-start = ((bf16[4,768,512]{1,2,0:T(8,128)(2,1)}), bf16[4,768,512]{1,2,0:T(8,128)(2,1)}, u32[]{:S(2)}, u32[]{:S(2)}) async-start(bf16[4,768,512]{1,2,0:T(8,128)(2,1)} %bitcast.78), calls=%async_computation | async-start | bytes 6291456 | tf_op jit(solution)/shard_map/all_to_all | solution.py:22
  165.5 11.4 %all_gather.26 = bf16[768,512]{1,0:T(8,128)(2,1)S(1)} all-gather(bf16[768,128]{1,0:T(8,128)(2,1)S(1)} %get-tuple-element.25), channel_id=1, replica_groups=mesh['pole'=4,'row'=2,'col'=4] {'pole'}, dimensions={1}, use_global_device_ids=true | all-gather | bytes 983040 | tf_op jit(solution)/shard_map/all_gather | solution.py:17
  176.9 12.1 %all_gather.25 = bf16[768,512]{1,0:T(8,128)(2,1)S(1)} all-gather(bf16[768,128]{1,0:T(8,128)(2,1)S(1)} %get-tuple-element.24), channel_id=1, replica_groups=mesh['pole'=4,'row'=2,'col'=4] {'pole'}, dimensions={1}, use_global_device_ids=true | all-gather | bytes 983040 | tf_op jit(solution)/shard_map/all_gather | solution.py:16
  189.0 2.3 fusion.37
  191.3 2.3 fusion.39
  193.6 1.6 add_convert_fusion
  195.2 1.6 subtract_convert_fusion.4
  196.9 2.7 convert_reduce_fusion
  199.6 1.0 fusion.73
  200.7 1.0 convolution_add_fusion
  202.6 33.2 %all-to-all-done = bf16[4,768,512]{1,2,0:T(8,128)(2,1)} async-done(((bf16[4,768,512]{1,2,0:T(8,128)(2,1)}), bf16[4,768,512]{1,2,0:T(8,128)(2,1)}, u32[]{:S(2)}, u32[]{:S(2)}) %all-to-all-start) | async-done | bytes 3145760 | tf_op jit(solution)/shard_map/all_to_all | solution.py:22
  235.9 2.6 convert_reduce_fusion.1
  238.4 1.0 fusion.76
  239.6 1.0 convolution_add_fusion.1
  241.7 1.3 copy.22
  243.0 29.8 %all_to_all.25 = bf16[8,128,512]{2,1,0:T(8,128)(2,1)S(1)} all-to-all(bf16[8,128,512]{2,1,0:T(8,128)(2,1)} %bitcast.81), channel_id=1, replica_groups=mesh['pole'=4,'row'=2,'col'=4] {'row','col'}, dimensions={0} | all-to-all | bytes 2097152 | tf_op jit(solution)/shard_map/all_to_all | solution.py:22
  274.2 4.4 %fusion.28 = f32[768,1,512]{0,2,1:T(8,128)} fusion(f32[768,2,256]{0,2,1:T(8,128)} %bitcast.74, f32[768,2,256]{0,2,1:T(8,128)} %bitcast.72, f32[]{:T(128)} %bitcast.18, f32[]{:T(128)} %bitcast.17), kind=kLoop, calls=%fused_computation.41 | loop fusion | flops 1966080 | bytes 4718600 | tf_op jit(solution)/shard_map/sub | solution.py:90
  278.7 3.1 copy.23
  281.8 4.4 %all-to-all-start.3 = ((f32[4,768,128]{2,1,0:T(8,128)}), f32[4,768,128]{2,1,0:T(8,128)}, u32[]{:S(2)}, u32[]{:S(2)}) async-start(f32[4,768,128]{2,1,0:T(8,128)} %copy.23), calls=%async_computation.3 | async-start | bytes 3145728 | tf_op jit(solution)/shard_map/all_to_all | solution.py:22
  286.1 8.5 %all-gather.8.cloned.1.call-done = bf16[1024,512]{1,0:T(8,128)(2,1)} async-done(((bf16[128,512]{1,0:T(8,128)(2,1)}), bf16[1024,512]{1,0:T(8,128)(2,1)}) %all-gather.8.cloned.1.call-update) | async-done | bytes 1048592 | tf_op jit(solution)/shard_map/all_gather | solution.py:88
  294.6 1.5 convert_element_type.115
  297.5 2.5 fusion.43
  300.0 6.3 %all-to-all-done.3 = f32[4,768,128]{2,1,0:T(8,128)} async-done(((f32[4,768,128]{2,1,0:T(8,128)}), f32[4,768,128]{2,1,0:T(8,128)}, u32[]{:S(2)}, u32[]{:S(2)}) %all-to-all-start.3) | async-done | bytes 1572896 | tf_op jit(solution)/shard_map/all_to_all | solution.py:22
  306.2 3.5 %all-to-all-start.4 = ((f32[4,128,512]{2,1,0:T(8,128)}), f32[4,128,512]{2,1,0:T(8,128)S(1)}, u32[]{:S(2)}, u32[]{:S(2)}) async-start(f32[4,128,512]{2,1,0:T(8,128)} %bitcast.23), calls=%async_computation.4 | async-start | bytes 2097152 | tf_op jit(solution)/shard_map/all_to_all | solution.py:22
  309.8 3.7 %fusion.19 = f32[1,768,2,512]{1,3,2,0:T(8,128)} fusion(f32[768,2,256]{0,2,1:T(8,128)} %bitcast.73, f32[768,2,256]{0,2,1:T(8,128)} %bitcast.75), kind=kLoop, calls=%fused_computation.22 | loop fusion | flops 786432 | bytes 6291456 | tf_op jit(solution)/shard_map/broadcast_in_dim | solution.py:95
  313.5 5.7 %copy.24 = f32[1,768,2,512]{3,2,1,0:T(2,128)} copy(f32[1,768,2,512]{1,3,2,0:T(8,128)} %fusion.19) | data formatting | bytes 6291456
  319.2 2.3 reduce_sum.48
  321.5 3.4 %sub.62 = f32[1,2,512,512]{3,2,1,0:T(8,128)} subtract(f32[1,2,512,512]{3,2,1,0:T(8,128)S(1)} %copy-done, f32[1,2,512,512]{3,2,1,0:T(8,128)} %bitcast.77) | non-fusion elementwise | flops 524288 | bytes 6291456 | tf_op jit(solution)/shard_map/sub | solution.py:89
  (42 shorter events, 10.0 us)
Async XLA Ops:
  7.2 17.4 %copy-start = (f32[1,2,512,512]{3,2,1,0:T(8,128)S(1)}, f32[1,2,512,512]{3,2,1,0:T(8,128)}, u32[]{:S(2)}) copy-start(f32[1,2,512,512]{3,2,1,0:T(8,128)} %param.10) | copy-start | bytes 6291460
  7.2 58.3 %all-gather.6.cloned.1.call-start = ((), (), s32[]{:S(2)}) async-start(), calls=%async_computation.6 | async-start | bytes 2359296 | tf_op jit(solution)/shard_map/all_gather | solution.py:60
  9.3 2.7 collective-permute-start
  65.5 1.9 copy-start.6
  84.6 76.2 %all-to-all-start.1 = ((bf16[4,768,512]{1,2,0:T(8,128)(2,1)}), bf16[4,768,512]{1,2,0:T(8,128)(2,1)}, u32[]{:S(2)}, u32[]{:S(2)}) async-start(bf16[4,768,512]{1,2,0:T(8,128)(2,1)} %bitcast.79), calls=%async_computation.1 | async-start | bytes 6291456 | tf_op jit(solution)/shard_map/all_to_all | solution.py:22
  89.4 14.2 %all-gather.4.cloned.1.call-start = ((), (), s32[]{:S(2)}) async-start(), calls=%async_computation.5 | async-start | bytes 2359296 | tf_op jit(solution)/shard_map/all_gather | solution.py:60
  103.7 1.9 copy-start.7
  160.8 75.1 %all-to-all-start = ((bf16[4,768,512]{1,2,0:T(8,128)(2,1)}), bf16[4,768,512]{1,2,0:T(8,128)(2,1)}, u32[]{:S(2)}, u32[]{:S(2)}) async-start(bf16[4,768,512]{1,2,0:T(8,128)(2,1)} %bitcast.78), calls=%async_computation | async-start | bytes 6291456 | tf_op jit(solution)/shard_map/all_to_all | solution.py:22
  165.4 129.2 %all-gather.8.cloned.1.call-start = ((), (), s32[]{:S(2)}) async-start(), calls=%async_computation.7 | async-start | bytes 1179648 | tf_op jit(solution)/shard_map/all_gather | solution.py:88
  196.9 3.7 %copy-start.3 = (bf16[768,512]{0,1:T(8,128)(2,1)}, bf16[768,512]{0,1:T(8,128)(2,1)S(1)}, u32[]{:S(2)}) copy-start(bf16[768,512]{0,1:T(8,128)(2,1)S(1)} %subtract_convert_fusion.4) | copy-start | bytes 2359300
  199.6 1.1 copy-start.1
  235.9 2.6 copy-start.4
  238.4 1.2 copy-start.2
  240.6 1.0 copy-start.8
  243.0 30.6 %copy-start.9 = (f32[1,2]{1,0:T(1,128)S(1)}, f32[1,2]{1,0:T(1,128)}, u32[]{:S(2)}) copy-start(f32[1,2]{1,0:T(1,128)} %param.9) | copy-start | bytes 28
  281.8 24.5 %all-to-all-start.3 = ((f32[4,768,128]{2,1,0:T(8,128)}), f32[4,768,128]{2,1,0:T(8,128)}, u32[]{:S(2)}, u32[]{:S(2)}) async-start(f32[4,768,128]{2,1,0:T(8,128)} %copy.23), calls=%async_computation.3 | async-start | bytes 3145728 | tf_op jit(solution)/shard_map/all_to_all | solution.py:22
  296.2 1.3 copy-start.5
  306.2 18.7 %all-to-all-start.4 = ((f32[4,128,512]{2,1,0:T(8,128)}), f32[4,128,512]{2,1,0:T(8,128)S(1)}, u32[]{:S(2)}, u32[]{:S(2)}) async-start(f32[4,128,512]{2,1,0:T(8,128)} %bitcast.23), calls=%async_computation.4 | async-start | bytes 2097152 | tf_op jit(solution)/shard_map/all_to_all | solution.py:22
Sparse Core Ops, SparseCore 0:
  45.8 19.6 all-gather.5
  92.4 11.2 all-gather.3
  273.7 20.8 all-gather.7
where the time goes:
time: 333 us; the launch traced here: 332 us
  waiting for transfers between devices  119 us (36%)
  blocking collectives  78.1 us (23%)
  matrix products  50.3 us (15%)
  other arithmetic  31.3 us (9%)
  local copies, waits for them, and re-layouts  20.5 us (6%)
  starting transfers between devices  18.2 us (5%)
  between operations  14.7 us (4%)
    all_to_all x4, waiting for transfers between devices, exchange_sum(): lax.all_to_all(pieces, axis, 0, 0, tiled=True).astype(jnp.float32)  77.5 us
    all_gather x2, waiting for transfers between devices, body(): rows = lax.all_gather(mine, 'row', axis=0, tiled=True)  33.1 us
    all_to_all x1, blocking collectives, exchange_sum(): lax.all_to_all(pieces, axis, 0, 0, tiled=True).astype(jnp.float32)  29.8 us
    all_gather x2, blocking collectives, gather_panel(): lax.all_gather(pair[:rows], 'pole', axis=1, tiled=True)  24.3 us
    all_gather x2, blocking collectives, gather_panel(): lax.all_gather(pair[rows:], 'pole', axis=1, tiled=True)  24 us
    all_to_all x4, starting transfers between devices, exchange_sum(): lax.all_to_all(pieces, axis, 0, 0, tiled=True).astype(jnp.float32)  17.4 us
    dot_general x8, matrix products, precise(): jnp.dot(left, right, precision=lax.Precision.HIGH, preferred_element_type...  15.6 us
    dot_general x2, matrix products, body(): jnp.dot(block_real, rows, preferred_element_type=jnp.float32)  15.3 us
  transfers between devices with their start and end apart: 8, of which 6 were waited for; matrix products, arithmetic and copies ran while one was open for 19% of the time, Pallas kernels for 0%

commit v1 on v0

--- a/solution.py
+++ b/solution.py
@@ -39,6 +39,22 @@
 
 
 def body(hamiltonian_panel, margin_panel, shifts, weights, pivot_inverse, selected_inverse):
+
+    def see_the_strips_all(row_data):
+        extent = lax.psum(1, axis_name=("row", "col"))
+        runs = [(k0, (k0 + 1) % extent) for k0 in range(extent)]
+        sheets = [(k0, (k0 - 1) % extent) for k0 in range(extent)]
+        wide_out, back = ([row_data], [row_data])
+        for _ in range(extent // 2):
+            wide_out.append(lax.ppermute(wide_out[-1], axis_name=("row", "col"), perm=runs))
+        for _ in tuple(range((extent - 1) // 2)):
+            back.append(lax.ppermute(back[-1], axis_name=("row", "col"), perm=sheets))
+        m_next = jnp.concatenate([*wide_out[::-1], *back[1:]], axis=0)
+        p_next = jnp.roll(
+            m_next, (lax.axis_index(("row", "col")) - extent // 2) * row_data.shape[0], axis=0
+        )
+        return p_next
+
     shift = shifts[0]
     weight = weights[0]
     inverse = pivot_inverse[0]
@@ -85,7 +101,7 @@
     update = jnp.concatenate(updates, axis=2)
     pieces = update.reshape(n_row * n_col, -1, width).astype(jnp.bfloat16)
     piece = lax.optimization_barrier(exchange_sum(pieces, ("row", "col")))
-    update = lax.all_gather(piece.astype(jnp.bfloat16), ("row", "col"), axis=0, tiled=True)
+    update = see_the_strips_all(piece.astype(jnp.bfloat16))
     pivot = inverse - update.reshape(2, width, width).astype(jnp.float32)
     column_density = weight[0] * column[:, 0] - weight[1] * column[:, 1]
     share = width // n_pole

time: 333 us -> 355 us (1.066)
  waiting for transfers between devices: 119 us -> 131 us
  starting transfers between devices: 18.2 us -> 28.6 us
    ppermute x0 -> x7, waiting for transfers between devices: none -> 18.3 us  [the longest x4 14.3 us: see_the_strips_all(): lax.ppermute(wide_out[-1], axis_name=('row', 'col'), perm=runs)]
    ppermute x0 -> x7, starting transfers between devices: none -> 10.5 us  [the longest x3 10.4 us: see_the_strips_all(): back.append(lax.ppermute(back[-1], axis_name=('row', 'col'), perm=sheets))]
    all_gather x1 -> x0, waiting for transfers between devices: 8.52 us -> none  [body(): lax.all_gather(piece.astype(jnp.bfloat16), ('row', 'col'), axis=0, tiled=...]
    unnamed x22 -> x37, local copies, waits for them, and re-layouts: 9.24 us -> 9.45 us
  transfers between devices with their start and end apart: 8 -> 14, of which waited for: 6 -> 10; matrix products, arithmetic and copies ran while one was open for 19% -> 17% of each run, Pallas kernels for 0% -> 0%
where the time goes in v1:
time: 355 us; the launch traced here: 354 us
  waiting for transfers between devices  131 us (37%)
  blocking collectives  78.1 us (22%)
  matrix products  50.3 us (14%)
  other arithmetic  29.4 us (8%)
  starting transfers between devices  28.6 us (8%)
  local copies, waits for them, and re-layouts  20.7 us (6%)
  between operations  15.1 us (4%)
    all_to_all x4, waiting for transfers between devices, exchange_sum(): lax.all_to_all(pieces, axis, 0, 0, tiled=True).astype(jnp.float32)  80.1 us
    all_gather x2, waiting for transfers between devices, body(): rows = lax.all_gather(mine, 'row', axis=0, tiled=True)  33.1 us
    all_to_all x1, blocking collectives, exchange_sum(): lax.all_to_all(pieces, axis, 0, 0, tiled=True).astype(jnp.float32)  29.8 us
    all_gather x2, blocking collectives, gather_panel(): lax.all_gather(pair[:rows], 'pole', axis=1, tiled=True)  24.3 us
    all_gather x2, blocking collectives, gather_panel(): lax.all_gather(pair[rows:], 'pole', axis=1, tiled=True)  24 us
    all_to_all x4, starting transfers between devices, exchange_sum(): lax.all_to_all(pieces, axis, 0, 0, tiled=True).astype(jnp.float32)  17.4 us
    dot_general x8, matrix products, precise(): jnp.dot(left, right, precision=lax.Precision.HIGH, preferred_element_type...  15.6 us
    dot_general x2, matrix products, body(): jnp.dot(block_real, rows, preferred_element_type=jnp.float32)  15.3 us
  transfers between devices with their start and end apart: 14, of which 10 were waited for; matrix products, arithmetic and copies ran while one was open for 17% of the time, Pallas kernels for 0%

profile of v1, /device:TPU:0, one launch (start us, length us, event | category | flops | bytes accessed | tf_op | source)
XLA Modules:
  0.0 353.7 jit_solution(4067947522591740570)
XLA Ops:
  10.0 1.3 fusion.91
  12.0 12.6 %all_gather.19 = bf16[768,512]{1,0:T(8,128)(2,1)S(1)} all-gather(bf16[768,128]{1,0:T(8,128)(2,1)S(1)} %get-tuple-element.27), channel_id=1, replica_groups=mesh['pole'=4,'row'=2,'col'=4] {'pole'}, dimensions={1}, use_global_device_ids=true | all-gather | bytes 983040 | tf_op jit(solution)/shard_map/all_gather | solution.py:17
  24.5 1.6 fusion.21
  26.2 1.6 fusion.20
  27.8 12.2 %all_gather.18 = bf16[768,512]{1,0:T(8,128)(2,1)S(1)} all-gather(bf16[768,128]{1,0:T(8,128)(2,1)S(1)} %get-tuple-element.26), channel_id=1, replica_groups=mesh['pole'=4,'row'=2,'col'=4] {'pole'}, dimensions={1}, use_global_device_ids=true | all-gather | bytes 983040 | tf_op jit(solution)/shard_map/all_gather | solution.py:16
  40.0 2.3 subtract_convert_fusion.5
  42.3 2.3 add_convert_fusion.1
  45.7 19.8 %all-gather.5.cloned.1.call-done = bf16[1536,512]{0,1:T(8,128)(2,1)} async-done(((bf16[768,512]{0,1:T(8,128)(2,1)}), bf16[1536,512]{0,1:T(8,128)(2,1)}) %all-gather.5.cloned.1.call-update) | async-done | bytes 1572880 | tf_op jit(solution)/shard_map/all_gather | solution.py:76
  65.5 1.6 fusion.85
  67.4 7.7 %fusion = f32[512,3072]{1,0:T(8,128)S(1)} fusion(bf16[1536,512]{0,1:T(8,128)(2,1)S(1)} %copy-done.6, bf16[1,2,3072,1536]{3,2,1,0:T(8,128)(2,1)} %param.11), kind=kOutput, calls=%fused_computation | convolution fusion | flops 4831838208 | bytes 17301504 | tf_op jit(solution)/shard_map/dot_general | solution.py:78
  75.1 7.6 %fusion.16 = bf16[3072,512]{0,1:T(8,128)(2,1)S(1)} fusion(f32[512,3072]{1,0:T(8,128)S(1)} %fusion, bf16[1,2,3072,1536]{3,2,1,0:T(8,128)(2,1)} %param.11, bf16[1536,256]{0,1:T(8,128)(2,1)S(1)} %get-tuple-element.19, bf16[1536,256]{0,1:T(8,128)(2,1)S(1)} %get-tuple-element.18), kind=kOutput, calls=%fused_computation.21 | convolution fusion | flops 4838129664 | bytes 20447232 | tf_op jit(solution)/shard_map/dot_general | solution.py:78
  82.7 1.9 copy.31
  84.6 4.9 %all-to-all-start.1 = ((bf16[4,768,512]{1,2,0:T(8,128)(2,1)}), bf16[4,768,512]{1,2,0:T(8,128)(2,1)}, u32[]{:S(2)}, u32[]{:S(2)}) async-start(bf16[4,768,512]{1,2,0:T(8,128)(2,1)} %bitcast.79), calls=%async_computation.1 | async-start | bytes 6291456 | tf_op jit(solution)/shard_map/all_to_all | solution.py:22
  90.4 13.2 %all-gather.3.cloned.1.call-done = bf16[1536,512]{0,1:T(8,128)(2,1)} async-done(((bf16[768,512]{0,1:T(8,128)(2,1)}), bf16[1536,512]{0,1:T(8,128)(2,1)}) %all-gather.3.cloned.1.call-update) | async-done | bytes 1572880 | tf_op jit(solution)/shard_map/all_gather | solution.py:76
  103.7 1.6 fusion.84
  105.5 7.7 %fusion.2 = f32[512,3072]{1,0:T(8,128)S(1)} fusion(bf16[1536,512]{0,1:T(8,128)(2,1)S(1)} %copy-done.7, bf16[1,2,3072,1536]{3,2,1,0:T(8,128)(2,1)} %param.11), kind=kOutput, calls=%fused_computation.2 | convolution fusion | flops 4831838208 | bytes 17301504 | tf_op jit(solution)/shard_map/dot_general | solution.py:78
  113.2 7.6 %subtract_convert_fusion.1 = bf16[512,3072]{1,0:T(8,128)(2,1)S(1)} fusion(f32[512,3072]{1,0:T(8,128)S(1)} %fusion.2, bf16[1,2,3072,1536]{3,2,1,0:T(8,128)(2,1)} %param.11, bf16[1536,256]{0,1:T(8,128)(2,1)S(1)} %get-tuple-element.17, bf16[1536,256]{0,1:T(8,128)(2,1)S(1)} %get-tuple-element.16), kind=kOutput, calls=%fused_computation.15 | convolution fusion | flops 4838129664 | bytes 20447232 | tf_op jit(solution)/shard_map/dot_general | solution.py:78
  120.9 1.9 copy.32
  122.8 38.0 %all-to-all-done.1 = bf16[4,768,512]{1,2,0:T(8,128)(2,1)} async-done(((bf16[4,768,512]{1,2,0:T(8,128)(2,1)}), bf16[4,768,512]{1,2,0:T(8,128)(2,1)}, u32[]{:S(2)}, u32[]{:S(2)}) %all-to-all-start.1) | async-done | bytes 3145760 | tf_op jit(solution)/shard_map/all_to_all | solution.py:22
  160.8 4.6 %all-to-all-start = ((bf16[4,768,512]{1,2,0:T(8,128)(2,1)}), bf16[4,768,512]{1,2,0:T(8,128)(2,1)}, u32[]{:S(2)}, u32[]{:S(2)}) async-start(bf16[4,768,512]{1,2,0:T(8,128)(2,1)} %bitcast.78), calls=%async_computation | async-start | bytes 6291456 | tf_op jit(solution)/shard_map/all_to_all | solution.py:22
  165.4 11.4 %all_gather.23 = bf16[768,512]{1,0:T(8,128)(2,1)S(1)} all-gather(bf16[768,128]{1,0:T(8,128)(2,1)S(1)} %get-tuple-element.25), channel_id=1, replica_groups=mesh['pole'=4,'row'=2,'col'=4] {'pole'}, dimensions={1}, use_global_device_ids=true | all-gather | bytes 983040 | tf_op jit(solution)/shard_map/all_gather | solution.py:17
  176.9 12.1 %all_gather.22 = bf16[768,512]{1,0:T(8,128)(2,1)S(1)} all-gather(bf16[768,128]{1,0:T(8,128)(2,1)S(1)} %get-tuple-element.24), channel_id=1, replica_groups=mesh['pole'=4,'row'=2,'col'=4] {'pole'}, dimensions={1}, use_global_device_ids=true | all-gather | bytes 983040 | tf_op jit(solution)/shard_map/all_gather | solution.py:16
  189.0 2.3 fusion.37
  191.3 2.3 fusion.39
  193.5 1.6 add_convert_fusion
  195.2 1.6 subtract_convert_fusion.4
  196.8 2.7 convert_reduce_fusion
  202.6 33.3 %all-to-all-done = bf16[4,768,512]{1,2,0:T(8,128)(2,1)} async-done(((bf16[4,768,512]{1,2,0:T(8,128)(2,1)}), bf16[4,768,512]{1,2,0:T(8,128)(2,1)}, u32[]{:S(2)}, u32[]{:S(2)}) %all-to-all-start) | async-done | bytes 3145760 | tf_op jit(solution)/shard_map/all_to_all | solution.py:22
  235.8 2.6 convert_reduce_fusion.1
  241.7 1.3 copy.22
  243.0 29.8 %all_to_all.25 = bf16[8,128,512]{2,1,0:T(8,128)(2,1)S(1)} all-to-all(bf16[8,128,512]{2,1,0:T(8,128)(2,1)} %bitcast.81), channel_id=1, replica_groups=mesh['pole'=4,'row'=2,'col'=4] {'row','col'}, dimensions={0} | all-to-all | bytes 2097152 | tf_op jit(solution)/shard_map/all_to_all | solution.py:22
  273.0 7.3 %collective-permute-done.1 = bf16[128,512]{1,0:T(8,128)(2,1)S(1)} collective-permute-done((bf16[128,512]{1,0:T(8,128)(2,1)S(1)}, bf16[128,512]{1,0:T(8,128)(2,1)S(1)}, u32[]{:S(2)}, u32[]{:S(2)}) %collective-permute-start.1) | collective-permute-done | bytes 131104 | tf_op jit(solution)/shard_map/ppermute | solution.py:49
  280.4 3.6 %collective-permute-start.5 = (bf16[128,512]{1,0:T(8,128)(2,1)S(1)}, bf16[128,512]{1,0:T(8,128)(2,1)S(1)}, u32[]{:S(2)}, u32[]{:S(2)}) collective-permute-start(bf16[128,512]{1,0:T(8,128)(2,1)S(1)} %convert_reduce_fusion.2), channel_id=1, source_target_pairs={{0,7},{1,0},{2,1},{3,2},{4,3},{5,4},{6,5},{7,6},{8,15},{9,8},{10,9... | collective-permute-start | bytes 393224 | tf_op jit(solution)/shard_map/ppermute | solution.py:51
  283.9 3.8 %collective-permute-done.2 = bf16[128,512]{1,0:T(8,128)(2,1)S(1)} collective-permute-done((bf16[128,512]{1,0:T(8,128)(2,1)S(1)}, bf16[128,512]{1,0:T(8,128)(2,1)S(1)}, u32[]{:S(2)}, u32[]{:S(2)}) %collective-permute-start.2) | collective-permute-done | bytes 131104 | tf_op jit(solution)/shard_map/ppermute | solution.py:49
  288.7 3.2 collective-permute-start.6
  291.9 3.2 collective-permute-done.3
  295.1 4.5 %fusion.28 = f32[768,1,512]{0,2,1:T(8,128)} fusion(f32[768,2,256]{0,2,1:T(8,128)} %bitcast.74, f32[768,2,256]{0,2,1:T(8,128)} %bitcast.72, f32[]{:T(128)} %bitcast.18, f32[]{:T(128)} %bitcast.17), kind=kLoop, calls=%fused_computation.41 | loop fusion | flops 1966080 | bytes 4718600 | tf_op jit(solution)/shard_map/sub | solution.py:106
  299.6 3.1 copy.23
  302.6 4.3 %all-to-all-start.3 = ((f32[4,768,128]{2,1,0:T(8,128)}), f32[4,768,128]{2,1,0:T(8,128)}, u32[]{:S(2)}, u32[]{:S(2)}) async-start(f32[4,768,128]{2,1,0:T(8,128)} %copy.23), calls=%async_computation.3 | async-start | bytes 3145728 | tf_op jit(solution)/shard_map/all_to_all | solution.py:22
  307.0 3.6 %collective-permute-start.7 = (bf16[128,512]{1,0:T(8,128)(2,1)S(1)}, bf16[128,512]{1,0:T(8,128)(2,1)S(1)}, u32[]{:S(2)}, u32[]{:S(2)}) collective-permute-start(bf16[128,512]{1,0:T(8,128)(2,1)S(1)} %collective-permute-done.6), channel_id=1, source_target_pairs={{0,7},{1,0},{2,1},{3,2},{4,3},{5,4},{6,5},{7,6},{8,15},{9,8},{10,9... | collective-permute-start | bytes 393224 | tf_op jit(solution)/shard_map/ppermute | solution.py:51
  310.7 3.6 %collective-permute-done.7 = bf16[128,512]{1,0:T(8,128)(2,1)S(1)} collective-permute-done((bf16[128,512]{1,0:T(8,128)(2,1)S(1)}, bf16[128,512]{1,0:T(8,128)(2,1)S(1)}, u32[]{:S(2)}, u32[]{:S(2)}) %collective-permute-start.7) | collective-permute-done | bytes 131104 | tf_op jit(solution)/shard_map/ppermute | solution.py:51
  316.1 2.5 fusion.43
  318.6 8.9 %all-to-all-done.3 = f32[4,768,128]{2,1,0:T(8,128)} async-done(((f32[4,768,128]{2,1,0:T(8,128)}), f32[4,768,128]{2,1,0:T(8,128)}, u32[]{:S(2)}, u32[]{:S(2)}) %all-to-all-start.3) | async-done | bytes 1572896 | tf_op jit(solution)/shard_map/all_to_all | solution.py:22
  327.5 3.5 all-to-all-start.4
  331.0 3.7 %fusion.19 = f32[1,768,2,512]{1,3,2,0:T(8,128)} fusion(f32[768,2,256]{0,2,1:T(8,128)} %bitcast.73, f32[768,2,256]{0,2,1:T(8,128)} %bitcast.75), kind=kLoop, calls=%fused_computation.22 | loop fusion | flops 786432 | bytes 6291456 | tf_op jit(solution)/shard_map/broadcast_in_dim | solution.py:111
  334.7 5.7 %copy.24 = f32[1,768,2,512]{3,2,1,0:T(2,128)} copy(f32[1,768,2,512]{1,3,2,0:T(8,128)} %fusion.19) | data formatting | bytes 6291456
  340.4 2.3 reduce_sum.48
  342.7 3.4 sub.71
  (69 shorter events, 15.4 us)
Async XLA Ops:
  7.2 17.4 %copy-start = (f32[1,2,512,512]{3,2,1,0:T(8,128)S(1)}, f32[1,2,512,512]{3,2,1,0:T(8,128)}, u32[]{:S(2)}) copy-start(f32[1,2,512,512]{3,2,1,0:T(8,128)} %param.10) | copy-start | bytes 6291460
  7.2 58.3 %all-gather.5.cloned.1.call-start = ((), (), s32[]{:S(2)}) async-start(), calls=%async_computation.6 | async-start | bytes 2359296 | tf_op jit(solution)/shard_map/all_gather | solution.py:76
  9.3 2.7 collective-permute-start
  65.5 1.9 copy-start.6
  84.6 76.2 %all-to-all-start.1 = ((bf16[4,768,512]{1,2,0:T(8,128)(2,1)}), bf16[4,768,512]{1,2,0:T(8,128)(2,1)}, u32[]{:S(2)}, u32[]{:S(2)}) async-start(bf16[4,768,512]{1,2,0:T(8,128)(2,1)} %bitcast.79), calls=%async_computation.1 | async-start | bytes 6291456 | tf_op jit(solution)/shard_map/all_to_all | solution.py:22
  89.4 14.2 %all-gather.3.cloned.1.call-start = ((), (), s32[]{:S(2)}) async-start(), calls=%async_computation.5 | async-start | bytes 2359296 | tf_op jit(solution)/shard_map/all_gather | solution.py:76
  103.7 1.9 copy-start.7
  160.8 75.1 %all-to-all-start = ((bf16[4,768,512]{1,2,0:T(8,128)(2,1)}), bf16[4,768,512]{1,2,0:T(8,128)(2,1)}, u32[]{:S(2)}, u32[]{:S(2)}) async-start(bf16[4,768,512]{1,2,0:T(8,128)(2,1)} %bitcast.78), calls=%async_computation | async-start | bytes 6291456 | tf_op jit(solution)/shard_map/all_to_all | solution.py:22
  196.8 3.7 %copy-start.3 = (bf16[768,512]{0,1:T(8,128)(2,1)}, bf16[768,512]{0,1:T(8,128)(2,1)S(1)}, u32[]{:S(2)}) copy-start(bf16[768,512]{0,1:T(8,128)(2,1)S(1)} %subtract_convert_fusion.4) | copy-start | bytes 2359300
  199.5 1.1 copy-start.1
  235.8 2.6 copy-start.4
  238.4 1.2 copy-start.2
  240.6 1.0 copy-start.8
  243.0 44.8 %copy-start.9 = (f32[1,2]{1,0:T(1,128)S(1)}, f32[1,2]{1,0:T(1,128)}, u32[]{:S(2)}) copy-start(f32[1,2]{1,0:T(1,128)} %param.9) | copy-start | bytes 28
  273.0 7.4 %collective-permute-start.1 = (bf16[128,512]{1,0:T(8,128)(2,1)S(1)}, bf16[128,512]{1,0:T(8,128)(2,1)S(1)}, u32[]{:S(2)}, u32[]{:S(2)}) collective-permute-start(bf16[128,512]{1,0:T(8,128)(2,1)S(1)} %convert_reduce_fusion.2), channel_id=1, source_target_pairs={{0,1},{1,2},{2,3},{3,4},{4,5},{5,6},{6,7},{7,0},{8,9},{9,10},{10,1... | collective-permute-start | bytes 393224 | tf_op jit(solution)/shard_map/ppermute | solution.py:49
  280.4 7.4 %collective-permute-start.2 = (bf16[128,512]{1,0:T(8,128)(2,1)S(1)}, bf16[128,512]{1,0:T(8,128)(2,1)S(1)}, u32[]{:S(2)}, u32[]{:S(2)}) collective-permute-start(bf16[128,512]{1,0:T(8,128)(2,1)S(1)} %collective-permute-done.1), channel_id=1, source_target_pairs={{0,1},{1,2},{2,3},{3,4},{4,5},{5,6},{6,7},{7,0},{8,9},{9,10},{10,1... | collective-permute-start | bytes 393224 | tf_op jit(solution)/shard_map/ppermute | solution.py:49
  280.4 8.3 %collective-permute-start.5 = (bf16[128,512]{1,0:T(8,128)(2,1)S(1)}, bf16[128,512]{1,0:T(8,128)(2,1)S(1)}, u32[]{:S(2)}, u32[]{:S(2)}) collective-permute-start(bf16[128,512]{1,0:T(8,128)(2,1)S(1)} %convert_reduce_fusion.2), channel_id=1, source_target_pairs={{0,7},{1,0},{2,1},{3,2},{4,3},{5,4},{6,5},{7,6},{8,15},{9,8},{10,9... | collective-permute-start | bytes 393224 | tf_op jit(solution)/shard_map/ppermute | solution.py:51
  287.8 7.3 %collective-permute-start.3 = (bf16[128,512]{1,0:T(8,128)(2,1)S(1)}, bf16[128,512]{1,0:T(8,128)(2,1)S(1)}, u32[]{:S(2)}, u32[]{:S(2)}) collective-permute-start(bf16[128,512]{1,0:T(8,128)(2,1)S(1)} %collective-permute-done.2), channel_id=1, source_target_pairs={{0,1},{1,2},{2,3},{3,4},{4,5},{5,6},{6,7},{7,0},{8,9},{9,10},{10,1... | collective-permute-start | bytes 393224 | tf_op jit(solution)/shard_map/ppermute | solution.py:49
  288.7 18.3 %collective-permute-start.6 = (bf16[128,512]{1,0:T(8,128)(2,1)S(1)}, bf16[128,512]{1,0:T(8,128)(2,1)S(1)}, u32[]{:S(2)}, u32[]{:S(2)}) collective-permute-start(bf16[128,512]{1,0:T(8,128)(2,1)S(1)} %collective-permute-done.5), channel_id=1, source_target_pairs={{0,7},{1,0},{2,1},{3,2},{4,3},{5,4},{6,5},{7,6},{8,15},{9,8},{10,9... | collective-permute-start | bytes 393224 | tf_op jit(solution)/shard_map/ppermute | solution.py:51
  295.1 15.5 %collective-permute-start.4 = (bf16[128,512]{1,0:T(8,128)(2,1)S(1)}, bf16[128,512]{1,0:T(8,128)(2,1)S(1)}, u32[]{:S(2)}, u32[]{:S(2)}) collective-permute-start(bf16[128,512]{1,0:T(8,128)(2,1)S(1)} %collective-permute-done.3), channel_id=1, source_target_pairs={{0,1},{1,2},{2,3},{3,4},{4,5},{5,6},{6,7},{7,0},{8,9},{9,10},{10,1... | collective-permute-start | bytes 393224 | tf_op jit(solution)/shard_map/ppermute | solution.py:49
  302.6 24.8 %all-to-all-start.3 = ((f32[4,768,128]{2,1,0:T(8,128)}), f32[4,768,128]{2,1,0:T(8,128)}, u32[]{:S(2)}, u32[]{:S(2)}) async-start(f32[4,768,128]{2,1,0:T(8,128)} %copy.23), calls=%async_computation.3 | async-start | bytes 3145728 | tf_op jit(solution)/shard_map/all_to_all | solution.py:22
  307.0 7.3 %collective-permute-start.7 = (bf16[128,512]{1,0:T(8,128)(2,1)S(1)}, bf16[128,512]{1,0:T(8,128)(2,1)S(1)}, u32[]{:S(2)}, u32[]{:S(2)}) collective-permute-start(bf16[128,512]{1,0:T(8,128)(2,1)S(1)} %collective-permute-done.6), channel_id=1, source_target_pairs={{0,7},{1,0},{2,1},{3,2},{4,3},{5,4},{6,5},{7,6},{8,15},{9,8},{10,9... | collective-permute-start | bytes 393224 | tf_op jit(solution)/shard_map/ppermute | solution.py:51
  314.8 1.3 copy-start.5
  327.5 18.6 %all-to-all-start.4 = ((f32[4,128,512]{2,1,0:T(8,128)}), f32[4,128,512]{2,1,0:T(8,128)S(1)}, u32[]{:S(2)}, u32[]{:S(2)}) async-start(f32[4,128,512]{2,1,0:T(8,128)} %bitcast.23), calls=%async_computation.4 | async-start | bytes 2097152 | tf_op jit(solution)/shard_map/all_to_all | solution.py:22
Sparse Core Ops, SparseCore 0:
  45.8 19.6 all-gather.4
  92.4 11.2 all-gather.2
